TPU v7x, 32 devices: a whole 2x2x4 slice. The times are simulated.
32 devices in a mesh: prow: 4 (over z), pcol: 8 (over y, x, core).
Axes of the slice: x: 2, y: 2, z: 4, core: 2. Of those that a mesh axis runs over, the one named last changes fastest.
Arguments:
- ancestor_inverse: float32 [16, 4, 128, 8, 8, 128], P(None, 'prow', None, None, 'pcol'), as said below
- panel: float32 [4, 16, 4, 128, 256], P(None, None, 'prow'), may hold values from -0.0625 to 0.0625
- pattern: int32 [4, 16, 4], replicated, may hold values 0 or 1
- diag_term: float32 [4, 256, 256], replicated, may hold values from -6 to 6
Outputs:
- block_column: float32 [4, 16, 4, 128, 256], P(None, 'pcol', 'prow')
- diag_block: float32 [4, 256, 256], replicated
Inputs may be any that keep to these rules, and one draw needn't show every extreme that they name: `ancestor_inverse`: A equals its transpose.
All inputs are finite; a program needn't handle non-finite values.
Results may differ from a plain program's by a relative error of at most 0.00007.
Values sent between devices are 32-bit elements; how exact they have to be, the bound alone decides.
A program may use at most 128 MiB of HBM per device.

v0:
```python
import jax
import jax.numpy as jnp
from jax import lax
from jax.sharding import PartitionSpec as P


def close_diagonal(partial_sum, diag_term):
    return diag_term - lax.psum(partial_sum, ("prow", "pcol"))


def cross_sum(left_rows, right_rows):
    return jnp.einsum("sbiw,sbiv->swv", left_rows, right_rows, precision=lax.Precision.HIGHEST)


def local(ancestor_inverse, panel, pattern, diag_term):
    grid_rows = lax.axis_size("prow")
    grid_cols = lax.axis_size("pcol")
    row_pos = lax.axis_index("prow")
    col_pos = lax.axis_index("pcol")
    node_count, row_blocks, _, block_size, node_width = panel.shape
    col_blocks = ancestor_inverse.shape[3]
    kept_blocks = row_blocks // grid_cols
    local_tile = ancestor_inverse.reshape(row_blocks * block_size, col_blocks * block_size)
    block_flags = pattern.astype(jnp.float32)
    own_flags = lax.dynamic_index_in_dim(block_flags, row_pos, 2, keepdims=False)
    masked_own = panel[:, :, 0] * own_flags[:, :, None, None]
    own_part = lax.dynamic_slice_in_dim(masked_own, col_pos * kept_blocks, kept_blocks, 1)
    spread = grid_cols // col_blocks
    group_pos = col_pos // grid_rows
    mirrored = jnp.einsum(
        "rk,srw->skw",
        local_tile,
        masked_own.reshape(node_count, row_blocks * block_size, node_width),
        precision=lax.Precision.HIGHEST,
    )
    mirrored = mirrored.reshape(node_count, col_blocks, 1, block_size, node_width)
    selector = (jnp.arange(spread) == group_pos // kept_blocks).astype(jnp.float32)
    outgoing_rows = (mirrored * selector[None, None, :, None, None]).reshape(
        node_count, grid_cols, block_size, node_width
    )
    received = lax.all_to_all(outgoing_rows, "pcol", split_axis=1, concat_axis=1, tiled=True)
    received = received.reshape(node_count, spread, kept_blocks, grid_rows, block_size, node_width)
    picked = lax.dynamic_index_in_dim(received, col_pos % spread, 1, keepdims=False)
    summed = lax.psum_scatter(picked, "prow", scatter_dimension=2, tiled=True)[:, :, 0]
    out_flags = lax.dynamic_slice_in_dim(own_flags, col_pos * kept_blocks, kept_blocks, 1)
    column_part = -(summed * out_flags[:, :, None, None])
    diag_block = close_diagonal(cross_sum(own_part, column_part), diag_term)
    return (column_part[:, :, None], diag_block)


def solution(mesh):
    in_specs = (
        P(None, "prow", None, None, "pcol", None),
        P(None, None, "prow", None, None),
        P(),
        P(),
    )
    out_specs = (P(None, "pcol", "prow", None, None), P())
    return jax.shard_map(local, mesh=mesh, in_specs=in_specs, out_specs=out_specs, check_vma=False)
```

profile of v0, /device:TPU:27, one launch (start us, length us, event | category | flops | bytes accessed | tf_op | source)
XLA Modules:
  0.0 431.9 jit_solution(11220142328376732817)
XLA Ops:
  7.2 0.0 all-reduce.6.cloned.1.call-start
  7.2 0.7 convert_element_type.7
  8.0 0.5 broadcast.20
  8.5 26.2 %reduce.3 = f32[16,128,8,128]{3,2,1,0:T(8,128)} reduce(f32[16,1,128,8,1,128]{5,4,3,2,1,0:T(1,128)} %param.4, f32[]{:T(128)} %broadcast.20), dimensions={1,4}, to_apply=%param.4.reduce_sub_computation.3 | reduce | bytes 16777220 | tf_op args[0]
  34.7 9.3 %reshape.36 = f32[2048,1024,1]{1,0,2:T(8,128)} reshape(f32[16,128,8,128]{3,2,1,0:T(8,128)} %reduce.3) | data formatting | bytes 16777216 | tf_op jit(solution)/shard_map/reshape | solution.py:23
  43.9 0.0 copy-start
  43.9 4.5 %broadcast_multiply_fusion = f32[4,16,1,128,256]{4,3,2,1,0:T(8,128)S(1)} fusion(f32[4,16,1,128,256]{4,3,2,1,0:T(8,128)} %param.5, f32[4,16]{1,0:T(4,128)S(1)} %bitcast.33), kind=kLoop, calls=%fused_computation.2 | loop fusion | flops 2097152 | bytes 16777472 | tf_op jit(solution)/shard_map/mul | solution.py:26
  48.4 1.3 copy-done
  49.7 27.6 %multiply_bitcast_fusion = f32[4,32,8,8,128]{4,3,2,1,0:T(8,128)S(1)} fusion(f32[4,2048,256]{2,1,0:T(8,128)S(1)} %bitcast.32, f32[2048,1024,1]{1,0,2:T(8,128)S(1)} %copy-done, f32[]{:T(128)S(6)} %convert_element_type.8), kind=kOutput, calls=%fused_computation.1 | convolution fusion | flops 25770852352 | bytes 20971524 | tf_op jit(solution)/shard_map/rk,srw->skw/dot_general | solution.py:30
  77.4 0.5 copy.25
  77.9 51.9 %all_to_all.5 = f32[4,8,128,256]{2,3,0,1:T(8,128)} all-to-all(f32[4,8,128,256]{2,3,0,1:T(8,128)S(1)} %bitcast.29), channel_id=1, replica_groups=mesh['prow'=4,'pcol'=8] {'pcol'}, dimensions={1} | all-to-all | bytes 8388608 | tf_op jit(solution)/shard_map/all_to_all | solution.py:41
  129.7 5.3 %copy.14 = f32[4,2,4,128,256]{4,3,2,1,0:T(8,128)} copy(f32[4,2,4,128,256]{3,4,0,2,1:T(8,128)} %bitcast.30) | data formatting | bytes 8388608 | tf_op jit(solution)/shard_map/jit(dynamic_index_in_dim)/squeeze | solution.py:43
  135.0 0.0 all-reduce.6.cloned.1.call-update
  135.0 0.0 all-reduce.4.cloned.1.call-start
  135.1 0.0 copy-start.2
  135.1 0.0 copy-start.1
  135.1 9.0 %copy.17 = f32[4,16,1,128,256]{3,4,1,0,2:T(8,128)} copy(f32[4,16,1,128,256]{4,3,2,1,0:T(8,128)} %param.5) | data formatting | bytes 16777216 | tf_op args[1]
  144.1 0.1 constant_dynamic-slice_fusion.1
  144.2 0.1 copy.15
  144.3 0.1 copy.16
  144.4 0.0 copy-done.2
  144.4 0.7 dynamic-slice.2
  145.0 0.1 constant_dynamic-slice_fusion
  145.1 143.2 %all-reduce.6.cloned.1.call-done = f32[4,2,4,128,256]{4,3,2,1,0:T(8,128)} async-done(((f32[4,2,4,128,256]{4,3,2,1,0:T(8,128)}), f32[4,2,4,128,256]{4,3,2,1,0:T(8,128)}) %all-reduce.6.cloned.1.call-update) | async-done | bytes 4194320
  288.3 4.5 %convolution_bitcast_fusion = f32[4,256,256]{2,1,0:T(8,128)} fusion(f32[4,16,128,256]{2,3,1,0:T(8,128)} %bitcast.31, s32[]{:T(128)S(6)} %select_n.29, f32[4,2,4,128,256]{4,3,2,1,0:T(8,128)} %all-reduce.6.cloned.1.call-done, u32[]{:T(128)} %bitcast.15, f32[4,2]{1,0:T(4,128)S(1)} %constant_dynamic-slice_fusion, f32[4,2]{1,0:T(4,128)S(1)} %copy.16), kind=kOutput, calls=%fused_computation.3 | convolution fusion | flops 806092800 | bytes 3146308 | tf_op jit(solution)/shard_map/sbiw,sbiv->swv/dot_general | solution.py:12
  292.8 0.0 all-reduce.4.cloned.1.call-update
  292.8 3.1 multiply_negate_fusion
  295.9 126.9 %all-reduce.4.cloned.1.call-done = f32[4,256,256]{2,1,0:T(8,128)} async-done(((f32[4,256,256]{2,1,0:T(8,128)}), f32[4,256,256]{2,1,0:T(8,128)}) %all-reduce.4.cloned.1.call-update) | async-done | bytes 1048592 | tf_op jit(solution)/shard_map/psum | solution.py:8
  422.7 0.0 copy-done.1
  422.7 2.3 sub.12
  (1 shorter events, 0.0 us)
Async XLA Ops:
  7.2 281.1 %all-reduce.6.cloned.1.call-start = ((), (), s32[]{:S(2)}) async-start(), calls=%async_computation.2 | async-start | bytes 8388608
  43.9 5.8 %copy-start = (f32[2048,1024,1]{1,0,2:T(8,128)S(1)}, f32[2048,1024,1]{1,0,2:T(8,128)}, u32[]{:S(2)}) copy-start(f32[2048,1024,1]{1,0,2:T(8,128)} %reshape.36) | copy-start | bytes 25165828
  135.0 287.7 %all-reduce.4.cloned.1.call-start = ((), (), s32[]{:S(2)}) async-start(), calls=%async_computation.1 | async-start | bytes 2097152 | tf_op jit(solution)/shard_map/psum | solution.py:8
  135.1 9.3 %copy-start.2 = (u32[32]{0:T(128)S(1)}, u32[32]{0:T(128)}, u32[]{:S(2)}) copy-start(u32[32]{0:T(128)} %constant.76) | copy-start | bytes 388
  135.1 287.6 %copy-start.1 = (f32[4,256,256]{2,1,0:T(8,128)S(1)}, f32[4,256,256]{2,1,0:T(8,128)}, u32[]{:S(2)}) copy-start(f32[4,256,256]{2,1,0:T(8,128)} %param.7) | copy-start | bytes 3145732
Sparse Core Ops, SparseCore 0:
  135.1 153.0 all-reduce.5
  294.9 127.8 all-reduce.3
where the time goes:
time: 437 us; the launch traced here: 432 us
  waiting for transfers between devices  270 us (62%)
  blocking collectives  51.9 us (12%)
  other arithmetic  36.8 us (8%)
  matrix products  32.2 us (7%)
  local copies, waits for them, and re-layouts  26.8 us (6%)
  between operations  14.1 us (3%)
    unnamed x3, waiting for transfers between devices  143 us
    psum x1, waiting for transfers between devices, close_diagonal(): return diag_term - lax.psum(partial_sum, ('prow', 'pcol'))  127 us
    all_to_all x1, blocking collectives, local(): lax.all_to_all(outgoing_rows, 'pcol', split_axis=1, concat_axis=1, tiled=...  51.9 us
    dot_general x1, matrix products, local(): jnp.einsum('rk,srw->skw', local_tile, masked_own.reshape(node_count, row_...  27.6 us
    unnamed x1, other arithmetic  26.2 us
    unnamed x9, local copies, waits for them, and re-layouts  11.4 us
    reshape x1, local copies, waits for them, and re-layouts, local(): ancestor_inverse.reshape(row_blocks * block_size, col_blocks * block_size)  9.27 us
  transfers between devices with their start and end apart: 2, of which 2 were waited for; matrix products, arithmetic and copies ran while one was open for 3% of the time, Pallas kernels for 0%

commit v1 on v0

v1 whole, which is shorter than its diff:
```python
import functools

import jax
import jax.numpy as jnp
from jax import lax
from jax.experimental import pallas as pl
from jax.experimental.pallas import tpu as pltpu
from jax.sharding import PartitionSpec as P

MESH = pl.DeviceIdType.MESH


def split(x):
    high = x.astype(jnp.bfloat16)
    return high, (x - high.astype(jnp.float32)).astype(jnp.bfloat16)


def tdot(left, right):
    return lax.dot_general(
        left, right, (((0,), (0,)), ((), ())), preferred_element_type=jnp.float32
    )


def kernel(
    grid_rows, grid_cols,
    tile_ref, panel_ref, pattern_ref, diag_ref,
    column_ref, out_ref,
    panel_high, panel_low, tiles, parts, received, cross, slices, sums, whole,
    tile_sem, send_sem, recv_sem, one_send, one_recv, two_send, two_recv, three_send, three_recv,
):
    row = lax.axis_index("prow")
    col = lax.axis_index("pcol")
    nodes, row_blocks, block, width = panel_ref.shape
    col_blocks = parts.shape[0]
    kept = row_blocks // grid_cols
    depth = row_blocks * block

    def turn(step):
        return lax.rem(step + col + 1, col_blocks)

    def fetch(step):
        slot = lax.rem(step, 2)
        return pltpu.make_async_copy(
            tile_ref.at[:, 0, :, turn(step), 0, :], tiles.at[slot], tile_sem.at[slot]
        )

    fetch(0).start()

    def prepare(flat, carry):
        node, b = flat // row_blocks, lax.rem(flat, row_blocks)
        flag = pattern_ref[node, b, row].astype(jnp.float32)
        high, low = split(panel_ref[node, b] * flag)
        panel_high[node, b] = high
        panel_low[node, b] = low
        return carry

    lax.fori_loop(0, nodes * row_blocks, prepare, 0)

    def send_copy(d):
        b = (d * grid_cols + col) // grid_rows
        owner_row, owner_col = lax.rem(col, grid_rows), b // kept
        slot = lax.rem(b, kept) * grid_rows + row
        copy = pltpu.make_async_remote_copy(
            src_ref=parts.at[d], dst_ref=received.at[slot],
            send_sem=send_sem.at[d], recv_sem=recv_sem.at[slot],
            device_id=(owner_row, owner_col), device_id_type=MESH,
        )
        mine = jnp.logical_and(owner_row == row, owner_col == col)
        return copy, mine, slot

    def produce(step, carry):
        d = turn(step)
        slot = lax.rem(step, 2)
        fetch(step).wait()

        @pl.when(step + 1 < col_blocks)
        def _():
            fetch(step + 1).start()

        high, low = split(tiles[slot].reshape(depth, block))
        both = jnp.concatenate([high, low], axis=1)

        def node_product(node, inner):
            upper = panel_high[node].reshape(depth, width)
            lower = panel_low[node].reshape(depth, width)
            double = tdot(both, upper)
            parts[d, node] = double[:block] + double[block:] + tdot(high, lower)
            return inner

        lax.fori_loop(0, nodes, node_product, 0)
        copy, mine, place = send_copy(d)

        @pl.when(jnp.logical_not(mine))
        def _():
            copy.start()

        @pl.when(mine)
        def _():
            received[place] = parts[d]

        return carry

    lax.fori_loop(0, col_blocks, produce, 0)

    def arrive(slot, carry):
        b = col * kept + slot // grid_rows
        source_col = lax.rem(b * grid_rows + row, grid_cols)
        source_row = lax.rem(slot, grid_rows)

        @pl.when(jnp.logical_not(jnp.logical_and(source_col == col, source_row == row)))
        def _():
            pltpu.make_async_remote_copy(
                src_ref=parts.at[0], dst_ref=received.at[slot],
                send_sem=send_sem.at[0], recv_sem=recv_sem.at[slot],
                device_id=(source_row, source_col), device_id_type=MESH,
            ).wait_recv()

        return carry

    lax.fori_loop(0, kept * grid_rows, arrive, 0)

    def close(node, carry):
        total = None
        for k in range(kept):
            b = col * kept + k
            value = received[k * grid_rows, node]
            for source in range(1, grid_rows):
                value = value + received[k * grid_rows + source, node]
            flag = pattern_ref[node, b, row].astype(jnp.float32)
            value = -(value * flag)
            column_ref[node, k] = value
            high, low = split(value)
            left_high, left_low = panel_high[node, b], panel_low[node, b]
            term = tdot(left_high, high) + tdot(left_high, low) + tdot(left_low, high)
            total = term if total is None else total + term
        cross[pl.ds(node * width, width), :] = total
        return carry

    lax.fori_loop(0, nodes, close, 0)

    share = nodes * width // grid_cols

    def piece(index):
        return pl.ds(pl.multiple_of(index * share, 8), share)

    def one(j):
        target = lax.rem(col + j, grid_cols)
        return pltpu.make_async_remote_copy(
            src_ref=cross.at[piece(target)], dst_ref=slices.at[j],
            send_sem=one_send.at[j], recv_sem=one_recv.at[j],
            device_id=(row, target), device_id_type=MESH,
        )

    def two(j):
        target = lax.rem(row + j, grid_rows)
        return pltpu.make_async_remote_copy(
            src_ref=sums.at[row], dst_ref=sums.at[row],
            send_sem=two_send.at[j], recv_sem=two_recv.at[j],
            device_id=(target, col), device_id_type=MESH,
        )

    def two_arrival(j):
        source = lax.rem(row - j + grid_rows, grid_rows)
        return pltpu.make_async_remote_copy(
            src_ref=sums.at[source], dst_ref=sums.at[source],
            send_sem=two_send.at[j], recv_sem=two_recv.at[j],
            device_id=(source, col), device_id_type=MESH,
        )

    def three(j):
        target = lax.rem(col + j, grid_cols)
        return pltpu.make_async_remote_copy(
            src_ref=whole.at[piece(col)], dst_ref=whole.at[piece(col)],
            send_sem=three_send.at[j], recv_sem=three_recv.at[j],
            device_id=(row, target), device_id_type=MESH,
        )

    def three_arrival(j):
        source = lax.rem(col - j + grid_cols, grid_cols)
        return pltpu.make_async_remote_copy(
            src_ref=whole.at[piece(source)], dst_ref=whole.at[piece(source)],
            send_sem=three_send.at[j], recv_sem=three_recv.at[j],
            device_id=(row, source), device_id_type=MESH,
        )

    def each(count, action):
        def body(j, carry):
            action(j)
            return carry

        lax.fori_loop(1, count, body, 0)

    each(grid_cols, lambda j: one(j).start())
    each(grid_cols, lambda j: one(j).wait_recv())
    value = cross[piece(col), :]
    for j in range(1, grid_cols):
        value = value + slices[j]
    sums[row] = value
    each(grid_rows, lambda j: two(j).start())
    each(grid_rows, lambda j: two_arrival(j).wait_recv())
    value = sums[0]
    for j in range(1, grid_rows):
        value = value + sums[j]
    whole[piece(col), :] = diag_ref[piece(col), :] - value
    each(grid_cols, lambda j: three(j).start())
    each(grid_cols, lambda j: three_arrival(j).wait_recv())
    out_ref[...] = whole[...]
    each(grid_cols, lambda j: one(j).wait_send())
    each(grid_rows, lambda j: two(j).wait_send())
    each(grid_cols, lambda j: three(j).wait_send())

    def leave(d, carry):
        copy, mine, _ = send_copy(d)

        @pl.when(jnp.logical_not(mine))
        def _():
            copy.wait_send()

        return carry

    lax.fori_loop(0, col_blocks, leave, 0)


def local(ancestor_inverse, panel, pattern, diag_term):
    grid_rows = lax.axis_size("prow")
    grid_cols = lax.axis_size("pcol")
    nodes, row_blocks, _, block, width = panel.shape
    col_blocks = ancestor_inverse.shape[3]
    kept = row_blocks // grid_cols
    f32 = jnp.float32
    share = nodes * width // grid_cols
    dma = pltpu.SemaphoreType.DMA
    vmem = pl.BlockSpec(memory_space=pltpu.VMEM)
    column, diag = pl.pallas_call(
        functools.partial(kernel, grid_rows, grid_cols),
        out_shape=(
            jax.ShapeDtypeStruct((nodes, kept, block, width), f32),
            jax.ShapeDtypeStruct((nodes * width, width), f32),
        ),
        in_specs=[
            pl.BlockSpec(memory_space=pl.ANY),
            vmem,
            pl.BlockSpec(memory_space=pltpu.SMEM),
            vmem,
        ],
        out_specs=(vmem, vmem),
        scratch_shapes=[
            pltpu.VMEM((nodes, row_blocks, block, width), jnp.bfloat16),
            pltpu.VMEM((nodes, row_blocks, block, width), jnp.bfloat16),
            pltpu.VMEM((2, row_blocks, block, block), f32),
            pltpu.VMEM((col_blocks, nodes, block, width), f32),
            pltpu.VMEM((kept * grid_rows, nodes, block, width), f32),
            pltpu.VMEM((nodes * width, width), f32),
            pltpu.VMEM((grid_cols, share, width), f32),
            pltpu.VMEM((grid_rows, share, width), f32),
            pltpu.VMEM((nodes * width, width), f32),
            dma((2,)),
            dma((col_blocks,)),
            dma((kept * grid_rows,)),
            dma((grid_cols,)),
            dma((grid_cols,)),
            dma((grid_rows,)),
            dma((grid_rows,)),
            dma((grid_cols,)),
            dma((grid_cols,)),
        ],
        compiler_params=pltpu.CompilerParams(
            has_side_effects=True, vmem_limit_bytes=52 * 1024 * 1024
        ),
    )(
        ancestor_inverse,
        panel.reshape(nodes, row_blocks, block, width),
        pattern,
        diag_term.reshape(nodes * width, width),
    )
    return column[:, :, None], diag.reshape(nodes, width, width)


def solution(mesh):
    in_specs = (
        P(None, "prow", None, None, "pcol", None),
        P(None, None, "prow", None, None),
        P(),
        P(),
    )
    out_specs = (P(None, "pcol", "prow", None, None), P())
    return jax.shard_map(local, mesh=mesh, in_specs=in_specs, out_specs=out_specs, check_vma=False)
```

time: 437 us -> 239 us (0.55)
  waiting for transfers between devices: 270 us -> 0 us
  Pallas kernels: 0 us -> 232 us
  blocking collectives: 51.9 us -> 0 us
  other arithmetic: 36.8 us -> 0 us
  matrix products: 32.2 us -> 0 us
  local copies, waits for them, and re-layouts: 26.8 us -> 4.05 us
  between operations: 14.1 us -> 0.64 us
    pallas_call x0 -> x1, Pallas kernels: none -> 232 us  [local(): pl.pallas_call(functools.partial(kernel, grid_rows, grid_cols), out_shape...]
    unnamed x3 -> x0, waiting for transfers between devices: 143 us -> none
    psum x1 -> x0, waiting for transfers between devices: 127 us -> none  [close_diagonal(): return diag_term - lax.psum(partial_sum, ('prow', 'pcol'))]
    all_to_all x1 -> x0, blocking collectives: 51.9 us -> none  [local(): lax.all_to_all(outgoing_rows, 'pcol', split_axis=1, concat_axis=1, tiled=...]
    dot_general x2 -> x0, matrix products: 32.2 us -> none  [the longest x1 27.6 us: local(): jnp.einsum('rk,srw->skw', local_tile, masked_own.reshape(node_count, row_...]
    unnamed x1 -> x0, other arithmetic: 26.2 us -> none
    reshape x1 -> x0, local copies, waits for them, and re-layouts: 9.27 us -> none  [local(): ancestor_inverse.reshape(row_blocks * block_size, col_blocks * block_size)]
    unnamed x9 -> x3, local copies, waits for them, and re-layouts: 11.4 us -> 4.05 us
  transfers between devices with their start and end apart: 2 -> 0, of which waited for: 2 -> 0; matrix products, arithmetic and copies ran while one was open for 3% -> 0% of each run, Pallas kernels for 0% -> 0%
where the time goes in v1:
time: 239 us; the launch traced here: 236 us
  Pallas kernels  232 us (97%)
  local copies, waits for them, and re-layouts  4.05 us (2%)
    pallas_call x1, Pallas kernels, local(): pl.pallas_call(functools.partial(kernel, grid_rows, grid_cols), out_shape...  232 us

profile of v1, /device:TPU:27, one launch (start us, length us, event | category | flops | bytes accessed | tf_op | source)
XLA Modules:
  0.0 236.4 jit_solution(12757786062311283744)
XLA Ops:
  0.6 0.8 copy.6.pattern_ref
  1.4 231.7 %shard_map.59 = (f32[4,2,128,256]{3,2,1,0:T(8,128)S(1)}, f32[1024,256]{1,0:T(8,128)}) custom-call(f32[16,1,128,8,1,128]{5,4,3,2,1,0:T(1,128)} %tile_ref.1, f32[4,16,128,256]{3,2,1,0:T(8,128)} %bitcast.7, s32[4,16,4]{2,1,0:T(8,128)S(1)} %copy.6.pattern_ref, f32[1024,256]{1,0:T(8,128)} %bitcast.8), custom_call_target="tpu_custom_call" | custom-call | tf_op jit(solution)/shard_map/pallas_call | solution.py:234
  233.1 1.0 copy.10
  234.1 2.3 copy.11

commit v2 on v1

--- a/solution.py
+++ b/solution.py
@@ -25,8 +25,8 @@
     grid_rows, grid_cols,
     tile_ref, panel_ref, pattern_ref, diag_ref,
     column_ref, out_ref,
-    panel_high, panel_low, tiles, parts, received, cross, slices, sums, whole,
-    tile_sem, send_sem, recv_sem, one_send, one_recv, two_send, two_recv, three_send, three_recv,
+    panel_high, panel_low, tiles, parts, received, inbox, cross, slices, sums, whole,
+    tile_sem, send_sem, recv_sem, hop_send, hop_recv, one_send, one_recv, two_send, two_recv, three_send, three_recv,
 ):
     row = lax.axis_index("prow")
     col = lax.axis_index("pcol")
@@ -58,15 +58,14 @@
 
     def send_copy(d):
         b = (d * grid_cols + col) // grid_rows
-        owner_row, owner_col = lax.rem(col, grid_rows), b // kept
-        slot = lax.rem(b, kept) * grid_rows + row
+        owner_col = b // kept
+        slot = lax.rem(b, kept) * grid_rows + lax.rem(col, grid_rows)
         copy = pltpu.make_async_remote_copy(
             src_ref=parts.at[d], dst_ref=received.at[slot],
             send_sem=send_sem.at[d], recv_sem=recv_sem.at[slot],
-            device_id=(owner_row, owner_col), device_id_type=MESH,
-        )
-        mine = jnp.logical_and(owner_row == row, owner_col == col)
-        return copy, mine, slot
+            device_id=(row, owner_col), device_id_type=MESH,
+        )
+        return copy, owner_col == col, slot
 
     def produce(step, carry):
         d = turn(step)
@@ -102,30 +101,79 @@
 
     lax.fori_loop(0, col_blocks, produce, 0)
 
-    def arrive(slot, carry):
-        b = col * kept + slot // grid_rows
-        source_col = lax.rem(b * grid_rows + row, grid_cols)
-        source_row = lax.rem(slot, grid_rows)
-
-        @pl.when(jnp.logical_not(jnp.logical_and(source_col == col, source_row == row)))
+    slots = kept * grid_rows
+
+    def hop(slot, side, target_row):
+        return pltpu.make_async_remote_copy(
+            src_ref=received.at[slot], dst_ref=inbox.at[side * slots + slot],
+            send_sem=hop_send.at[slot], recv_sem=hop_recv.at[side * slots + slot],
+            device_id=(target_row, col), device_id_type=MESH,
+        )
+
+    def absorb(slot, side, source_row):
+        hop(slot, side, source_row).wait_recv()
+
+        def add(node, carry):
+            received[slot, node] += inbox[side * slots + slot, node]
+            return carry
+
+        lax.fori_loop(0, nodes, add, 0)
+
+    def relay(index, carry):
+        turn_of, k = index // kept, lax.rem(index, kept)
+        half, low_end = turn_of // 2, lax.rem(turn_of, 2)
+        target = low_end * half + (1 - low_end) * (grid_rows - 1 - half)
+        slot = k * grid_rows + target
+        source_col = lax.rem((col * kept + k) * grid_rows + target, grid_cols)
+
+        @pl.when(source_col != col)
         def _():
             pltpu.make_async_remote_copy(
                 src_ref=parts.at[0], dst_ref=received.at[slot],
                 send_sem=send_sem.at[0], recv_sem=recv_sem.at[slot],
-                device_id=(source_row, source_col), device_id_type=MESH,
+                device_id=(row, source_col), device_id_type=MESH,
             ).wait_recv()
 
-        return carry
-
-    lax.fori_loop(0, kept * grid_rows, arrive, 0)
+        @pl.when(row < target)
+        def _():
+            @pl.when(row > 0)
+            def _():
+                absorb(slot, 0, row - 1)
+
+            hop(slot, 0, row + 1).start()
+
+        @pl.when(row > target)
+        def _():
+            @pl.when(row < grid_rows - 1)
+            def _():
+                absorb(slot, 1, row + 1)
+
+            hop(slot, 1, row - 1).start()
+
+        return carry
+
+    lax.fori_loop(0, slots, relay, 0)
+
+    def settle(k, carry):
+        slot = k * grid_rows + row
+
+        @pl.when(row > 0)
+        def _():
+            absorb(slot, 0, row - 1)
+
+        @pl.when(row < grid_rows - 1)
+        def _():
+            absorb(slot, 1, row + 1)
+
+        return carry
+
+    lax.fori_loop(0, kept, settle, 0)
 
     def close(node, carry):
         total = None
         for k in range(kept):
             b = col * kept + k
-            value = received[k * grid_rows, node]
-            for source in range(1, grid_rows):
-                value = value + received[k * grid_rows + source, node]
+            value = received[k * grid_rows + row, node]
             flag = pattern_ref[node, b, row].astype(jnp.float32)
             value = -(value * flag)
             column_ref[node, k] = value
@@ -219,6 +267,21 @@
         return carry
 
     lax.fori_loop(0, col_blocks, leave, 0)
+
+    def leave_hop(slot, carry):
+        target = lax.rem(slot, grid_rows)
+
+        @pl.when(row < target)
+        def _():
+            hop(slot, 0, row + 1).wait_send()
+
+        @pl.when(row > target)
+        def _():
+            hop(slot, 1, row - 1).wait_send()
+
+        return carry
+
+    lax.fori_loop(0, slots, leave_hop, 0)
 
 
 def local(ancestor_inverse, panel, pattern, diag_term):
@@ -250,6 +313,7 @@
             pltpu.VMEM((2, row_blocks, block, block), f32),
             pltpu.VMEM((col_blocks, nodes, block, width), f32),
             pltpu.VMEM((kept * grid_rows, nodes, block, width), f32),
+            pltpu.VMEM((2 * kept * grid_rows, nodes, block, width), f32),
             pltpu.VMEM((nodes * width, width), f32),
             pltpu.VMEM((grid_cols, share, width), f32),
             pltpu.VMEM((grid_rows, share, width), f32),
@@ -257,6 +321,8 @@
             dma((2,)),
             dma((col_blocks,)),
             dma((kept * grid_rows,)),
+            dma((kept * grid_rows,)),
+            dma((2 * kept * grid_rows,)),
             dma((grid_cols,)),
             dma((grid_cols,)),
             dma((grid_rows,)),

time: 239 us -> 177 us (0.74)
  Pallas kernels: 232 us -> 172 us
    pallas_call x1, Pallas kernels: 232 us -> 172 us  [local(): pl.pallas_call(functools.partial(kernel, grid_rows, grid_cols), out_shape...]
where the time goes in v2:
time: 177 us
  Pallas kernels  172 us (97%)
  local copies, waits for them, and re-layouts  4.05 us (2%)
    pallas_call x1, Pallas kernels, local(): pl.pallas_call(functools.partial(kernel, grid_rows, grid_cols), out_shape...  172 us
    unnamed x3, local copies, waits for them, and re-layouts  4.05 us

profile of v2, /device:TPU:27, one launch (start us, length us, event | category | flops | bytes accessed | tf_op | source)
XLA Modules:
  0.0 176.6 jit_solution(2429166728141728599)
XLA Ops:
  0.6 0.8 copy.6.pattern_ref
  1.4 172.0 %shard_map.59 = (f32[4,2,128,256]{3,2,1,0:T(8,128)S(1)}, f32[1024,256]{1,0:T(8,128)}) custom-call(f32[16,1,128,8,1,128]{5,4,3,2,1,0:T(1,128)} %tile_ref.1, f32[4,16,128,256]{3,2,1,0:T(8,128)} %bitcast.7, s32[4,16,4]{2,1,0:T(8,128)S(1)} %copy.6.pattern_ref, f32[1024,256]{1,0:T(8,128)} %bitcast.8), custom_call_target="tpu_custom_call" | custom-call | tf_op jit(solution)/shard_map/pallas_call | solution.py:297
  173.4 1.0 copy.10
  174.4 2.3 %copy.11 = f32[4,256,256]{2,1,0:T(8,128)} copy(f32[4,256,256]{2,1,0:T(8,128)} %bitcast.9) | data formatting | bytes 2097152

commit v3 on v2

--- a/solution.py
+++ b/solution.py
@@ -67,6 +67,57 @@
         )
         return copy, owner_col == col, slot
 
+    slots = kept * grid_rows
+    lag = 2
+
+    def hop(slot, side, target_row):
+        return pltpu.make_async_remote_copy(
+            src_ref=received.at[slot], dst_ref=inbox.at[side * slots + slot],
+            send_sem=hop_send.at[slot], recv_sem=hop_recv.at[side * slots + slot],
+            device_id=(target_row, col), device_id_type=MESH,
+        )
+
+    def absorb(slot, side, source_row):
+        hop(slot, side, source_row).wait_recv()
+
+        def add(node, carry):
+            received[slot, node] += inbox[side * slots + slot, node]
+            return carry
+
+        lax.fori_loop(0, nodes, add, 0)
+
+    def relay(index, carry):
+        first = (col * col_blocks) // grid_cols
+        slot = lax.rem(first - 1 - index + 2 * col_blocks, col_blocks)
+        k, target = slot // grid_rows, lax.rem(slot, grid_rows)
+        source_col = lax.rem((col * kept + k) * grid_rows + target, grid_cols)
+
+        @pl.when(source_col != col)
+        def _():
+            pltpu.make_async_remote_copy(
+                src_ref=parts.at[0], dst_ref=received.at[slot],
+                send_sem=send_sem.at[0], recv_sem=recv_sem.at[slot],
+                device_id=(row, source_col), device_id_type=MESH,
+            ).wait_recv()
+
+        @pl.when(row < target)
+        def _():
+            @pl.when(row > 0)
+            def _():
+                absorb(slot, 0, row - 1)
+
+            hop(slot, 0, row + 1).start()
+
+        @pl.when(row > target)
+        def _():
+            @pl.when(row < grid_rows - 1)
+            def _():
+                absorb(slot, 1, row + 1)
+
+            hop(slot, 1, row - 1).start()
+
+        return carry
+
     def produce(step, carry):
         d = turn(step)
         slot = lax.rem(step, 2)
@@ -97,62 +148,15 @@
         def _():
             received[place] = parts[d]
 
+        @pl.when(step >= lag)
+        def _():
+            relay(step - lag, 0)
+
         return carry
 
     lax.fori_loop(0, col_blocks, produce, 0)
 
-    slots = kept * grid_rows
-
-    def hop(slot, side, target_row):
-        return pltpu.make_async_remote_copy(
-            src_ref=received.at[slot], dst_ref=inbox.at[side * slots + slot],
-            send_sem=hop_send.at[slot], recv_sem=hop_recv.at[side * slots + slot],
-            device_id=(target_row, col), device_id_type=MESH,
-        )
-
-    def absorb(slot, side, source_row):
-        hop(slot, side, source_row).wait_recv()
-
-        def add(node, carry):
-            received[slot, node] += inbox[side * slots + slot, node]
-            return carry
-
-        lax.fori_loop(0, nodes, add, 0)
-
-    def relay(index, carry):
-        turn_of, k = index // kept, lax.rem(index, kept)
-        half, low_end = turn_of // 2, lax.rem(turn_of, 2)
-        target = low_end * half + (1 - low_end) * (grid_rows - 1 - half)
-        slot = k * grid_rows + target
-        source_col = lax.rem((col * kept + k) * grid_rows + target, grid_cols)
-
-        @pl.when(source_col != col)
-        def _():
-            pltpu.make_async_remote_copy(
-                src_ref=parts.at[0], dst_ref=received.at[slot],
-                send_sem=send_sem.at[0], recv_sem=recv_sem.at[slot],
-                device_id=(row, source_col), device_id_type=MESH,
-            ).wait_recv()
-
-        @pl.when(row < target)
-        def _():
-            @pl.when(row > 0)
-            def _():
-                absorb(slot, 0, row - 1)
-
-            hop(slot, 0, row + 1).start()
-
-        @pl.when(row > target)
-        def _():
-            @pl.when(row < grid_rows - 1)
-            def _():
-                absorb(slot, 1, row + 1)
-
-            hop(slot, 1, row - 1).start()
-
-        return carry
-
-    lax.fori_loop(0, slots, relay, 0)
+    lax.fori_loop(slots - lag, slots, relay, 0)
 
     def settle(k, carry):
         slot = k * grid_rows + row

time: 177 us -> 158 us (0.89)
  Pallas kernels: 172 us -> 153 us
    pallas_call x1, Pallas kernels: 172 us -> 153 us  [local(): pl.pallas_call(functools.partial(kernel, grid_rows, grid_cols), out_shape...]
where the time goes in v3:
time: 158 us
  Pallas kernels  153 us (97%)
  local copies, waits for them, and re-layouts  4.05 us (3%)
    pallas_call x1, Pallas kernels, local(): pl.pallas_call(functools.partial(kernel, grid_rows, grid_cols), out_shape...  153 us
    unnamed x3, local copies, waits for them, and re-layouts  4.05 us

profile of v3, /device:TPU:27, one launch (start us, length us, event | category | flops | bytes accessed | tf_op | source)
XLA Modules:
  0.0 157.6 jit_solution(3353028161153389290)
XLA Ops:
  0.6 0.8 copy.6.pattern_ref
  1.4 152.9 %shard_map.59 = (f32[4,2,128,256]{3,2,1,0:T(8,128)S(1)}, f32[1024,256]{1,0:T(8,128)}) custom-call(f32[16,1,128,8,1,128]{5,4,3,2,1,0:T(1,128)} %tile_ref.1, f32[4,16,128,256]{3,2,1,0:T(8,128)} %bitcast.7, s32[4,16,4]{2,1,0:T(8,128)S(1)} %copy.6.pattern_ref, f32[1024,256]{1,0:T(8,128)} %bitcast.8), custom_call_target="tpu_custom_call" | custom-call | tf_op jit(solution)/shard_map/pallas_call | solution.py:301
  154.3 1.0 copy.10
  155.3 2.3 %copy.11 = f32[4,256,256]{2,1,0:T(8,128)} copy(f32[4,256,256]{2,1,0:T(8,128)} %bitcast.9) | data formatting | bytes 2097152

commit v4 on v3

--- a/solution.py
+++ b/solution.py
@@ -127,14 +127,16 @@
         def _():
             fetch(step + 1).start()
 
-        high, low = split(tiles[slot].reshape(depth, block))
-        both = jnp.concatenate([high, low], axis=1)
+        high, low = split(tiles[slot].reshape(depth, block).T)
+        both = jnp.concatenate([high, low], axis=0)
 
         def node_product(node, inner):
             upper = panel_high[node].reshape(depth, width)
             lower = panel_low[node].reshape(depth, width)
-            double = tdot(both, upper)
-            parts[d, node] = double[:block] + double[block:] + tdot(high, lower)
+            double = jnp.dot(both, upper, preferred_element_type=jnp.float32)
+            parts[d, node] = double[:block] + double[block:] + jnp.dot(
+                high, lower, preferred_element_type=jnp.float32
+            )
             return inner
 
         lax.fori_loop(0, nodes, node_product, 0)

time: 158 us -> 158 us (level)
  no operation moved by 1% of the time
where the time goes in v4:
time: 158 us
  Pallas kernels  153 us (97%)
  local copies, waits for them, and re-layouts  4.05 us (3%)
    pallas_call x1, Pallas kernels, local(): pl.pallas_call(functools.partial(kernel, grid_rows, grid_cols), out_shape...  153 us
    unnamed x3, local copies, waits for them, and re-layouts  4.05 us

profile of v4, /device:TPU:27, one launch (start us, length us, event | category | flops | bytes accessed | tf_op | source)
XLA Modules:
  0.0 157.6 jit_solution(2720739562603510943)
XLA Ops:
  0.6 0.8 copy.6.pattern_ref
  1.4 152.9 %shard_map.59 = (f32[4,2,128,256]{3,2,1,0:T(8,128)S(1)}, f32[1024,256]{1,0:T(8,128)}) custom-call(f32[16,1,128,8,1,128]{5,4,3,2,1,0:T(1,128)} %tile_ref.1, f32[4,16,128,256]{3,2,1,0:T(8,128)} %bitcast.7, s32[4,16,4]{2,1,0:T(8,128)S(1)} %copy.6.pattern_ref, f32[1024,256]{1,0:T(8,128)} %bitcast.8), custom_call_target="tpu_custom_call" | custom-call | tf_op jit(solution)/shard_map/pallas_call | solution.py:303
  154.3 1.0 copy.10
  155.3 2.3 %copy.11 = f32[4,256,256]{2,1,0:T(8,128)} copy(f32[4,256,256]{2,1,0:T(8,128)} %bitcast.9) | data formatting | bytes 2097152
